TPU v7x, 512 devices: a whole 4x4x16 slice. The times are simulated.
512 devices in a mesh: alpha: 16 (over y, x), beta: 32 (over z, core).
Axes of the slice: x: 4, y: 4, z: 16, core: 2. Of those that a mesh axis runs over, the one named last changes fastest.
Arguments:
- coeffs: bfloat16 [2048, 4096], P('alpha', 'beta'), may hold values from -6 to 6
- send_rows: int32 [256, 32], P('alpha'), may hold values from 0 to 127
- alpha_source: int32 [256, 2048], P(None, 'alpha'), may hold values from 0 to 511
- alpha_sign: int32 [256, 2048], P(None, 'alpha'), may hold values from -1 to 1, as said below
- beta_source: int32 [256, 4096], P('beta'), may hold values from 0 to 4095
- beta_sign: int32 [256, 4096], P('beta'), may hold values from -1 to 1, as said below
- integrals: bfloat16 [256, 256], replicated, may hold values from -0.0234375 to 0.0234375
Outputs:
- sigma: bfloat16 [2048, 4096], P('alpha', 'beta')
Inputs may be any that keep to these rules, and one draw needn't show every extreme that they name: `alpha_sign`: each sign is -1 or 1. `beta_sign`: each sign is -1 or 1.
All inputs are finite; a program needn't handle non-finite values.
Results may differ from a plain program's by a relative error of at most 0.0049.
Values may be sent and summed in bfloat16 or wider, within the bound.
A program may use at most 64 MiB of HBM per device.

v0:
```python
import jax
import jax.numpy as jnp
from jax import lax
from jax.sharding import PartitionSpec as P


def take_rows(table, picks):
    return jnp.take(table, picks, axis=0)


def body(coeffs, send_rows, alpha_source, alpha_sign, beta_source, beta_sign, integrals):
    columns = coeffs.shape[1]
    picked = coeffs[send_rows]
    received = lax.all_to_all(picked, "alpha", split_axis=0, concat_axis=0, tiled=True)
    partner_table = received.reshape(-1, columns)
    slots = partner_table.shape[0]
    slot_ids = jnp.arange(slots, dtype=jnp.int32)
    selector = jnp.where(
        alpha_source[:, :, None] == slot_ids[None, None, :], alpha_sign[:, :, None], 0
    ).astype(jnp.bfloat16)
    excited = jnp.einsum(
        "qrs,sc->qrc", selector, partner_table, preferred_element_type=jnp.float32
    ).astype(jnp.bfloat16)
    mixed = jnp.einsum(
        "pq,qrc->prc", integrals, excited, preferred_element_type=jnp.float32
    ).astype(jnp.bfloat16)
    sign_local = beta_sign.astype(jnp.bfloat16)
    regrouped = lax.all_to_all(mixed, "beta", split_axis=0, concat_axis=2, tiled=True)
    turned = jnp.swapaxes(regrouped, 1, 2)
    moved = jax.vmap(take_rows)(turned, beta_source)
    terms = jnp.einsum("gcr,gc->rc", moved, sign_local, preferred_element_type=jnp.float32)
    return lax.psum_scatter(terms, "beta", scatter_dimension=1, tiled=True).astype(jnp.bfloat16)


def solution(mesh):
    in_specs = (
        P("alpha", "beta"),
        P("alpha", None),
        P(None, "alpha"),
        P(None, "alpha"),
        P("beta", None),
        P("beta", None),
        P(),
    )
    out_specs = P("alpha", "beta")
    return jax.shard_map(body, mesh=mesh, in_specs=in_specs, out_specs=out_specs, check_vma=False)
```

profile of v0, /device:TPU:1, one launch (start us, length us, event | category | flops | bytes accessed | tf_op | source)
XLA Modules:
  0.0 1099.6 jit_solution(1441012623883178677)
XLA Ops:
  6.5 0.0 copy-start
  6.5 0.7 compare_select_fusion.1
  7.3 0.1 reshape.13
  7.4 2.4 gather_fusion
  9.8 7.6 all-to-all-start
  17.4 1.0 copy.11
  18.4 1.0 copy.12
  19.4 4.8 all-to-all-done
  24.2 0.0 copy-done
  24.2 15.5 %convert_bitcast_fusion = bf16[256,128,128]{0,2,1:T(8,128)(2,1)} fusion(bf16[512,128,1]{1,0,2:T(8,128)(2,1)S(1)} %bitcast.38, s32[256,128]{0,1:T(8,128)S(1)} %copy.12, s32[256,128]{0,1:T(8,128)S(1)} %copy.11, bf16[256,256]{1,0:T(8,128)(2,1)S(1)} %copy-done), kind=kOutput, calls=%fused_computation.9 | convolution fusion | flops 6501171200 | bytes 8912896 | tf_op jit(solution)/shard_map/pq,qrc->prc/dot_general | solution.py:24
  39.7 12.4 %copy.14 = bf16[256,128,128]{2,1,0:T(8,128)(2,1)} copy(bf16[256,128,128]{0,2,1:T(8,128)(2,1)} %convert_bitcast_fusion) | data formatting | bytes 16777216 | tf_op jit(solution)/shard_map/convert_element_type | solution.py:26
  52.1 0.0 copy-start.1
  52.1 0.0 copy-start.2
  52.1 17.5 %all-to-all-start.1 = ((bf16[256,128,128]{2,1,0:T(8,128)(2,1)}), bf16[256,128,128]{2,1,0:T(8,128)(2,1)}, u32[]{:S(2)}, u32[]{:S(2)}) async-start(bf16[256,128,128]{2,1,0:T(8,128)(2,1)} %copy.14), calls=%async_computation.1 | async-start | bytes 16777216 | tf_op jit(solution)/shard_map/all_to_all | solution.py:28
  69.7 0.0 reduce-scatter.2.cloned.1.call-start
  69.7 0.0 copy-done.1
  69.8 0.0 copy-done.2
  69.9 360.4 %all-to-all-done.1 = bf16[256,128,128]{2,1,0:T(8,128)(2,1)} async-done(((bf16[256,128,128]{2,1,0:T(8,128)(2,1)}), bf16[256,128,128]{2,1,0:T(8,128)(2,1)}, u32[]{:S(2)}, u32[]{:S(2)}) %all-to-all-start.1) | async-done | bytes 8388640 | tf_op jit(solution)/shard_map/all_to_all | solution.py:28
  430.3 11.9 %copy.15 = bf16[8,128,32,128]{1,3,2,0:T(8,128)(2,1)} copy(bf16[8,128,32,128]{3,1,0,2:T(8,128)(2,1)} %bitcast.8) | data formatting | bytes 16777216 | tf_op jit(solution)/shard_map/all_to_all | solution.py:28
  442.2 529.6 %gather_fusion.1 = bf16[32768,128]{1,0:T(8,128)(2,1)} fusion(bf16[8,4096,128]{2,1,0:T(8,128)(2,1)} %bitcast.35, s32[32768]{0:T(1024)S(1)} %bitcast.34), kind=kCustom, calls=%fused_computation.1 | custom fusion | bytes 17039360 | tf_op jit(solution)/shard_map/vmap(jit(_take))/gather | solution.py:8
  971.8 12.6 %multiply_reduce_fusion = f32[4096,128]{1,0:T(8,128)S(1)} fusion(f32[4096,8]{0,1:T(8,128)S(1)} %bitcast_convert_fusion, bf16[8,4096,128]{2,1,0:T(8,128)(2,1)} %bitcast.36, pred[8,4096]{1,0:T(8,128)(4,1)S(1)} %compare_and_fusion), kind=kLoop, calls=%fused_computation.8 | loop fusion | flops 16252928 | bytes 10649600
  984.4 1.9 copy.23
  986.2 0.0 reduce-scatter.2.cloned.1.call-update
  986.3 105.0 %reduce-scatter.2.cloned.1.call-done = f32[128,128]{1,0:T(8,128)} async-done(((f32[128,4096]{1,0:T(8,128)}), f32[128,128]{1,0:T(8,128)}) %reduce-scatter.2.cloned.1.call-update) | async-done | bytes 65552 | tf_op jit(solution)/shard_map/reduce_scatter | solution.py:32
  1091.3 1.5 convert_element_type.23
  (5 shorter events, 0.1 us)
Async XLA Ops:
  6.5 17.7 %copy-start = (bf16[256,256]{1,0:T(8,128)(2,1)S(1)}, bf16[256,256]{1,0:T(8,128)(2,1)}, u32[]{:S(2)}) copy-start(bf16[256,256]{1,0:T(8,128)(2,1)} %param.13) | copy-start | bytes 393220
  9.8 14.4 %all-to-all-start = ((bf16[16,32,128]{2,1,0:T(8,128)(2,1)}), bf16[16,32,128]{2,1,0:T(8,128)(2,1)S(1)}, u32[]{:S(2)}, u32[]{:S(2)}) async-start(bf16[16,32,128]{2,1,0:T(8,128)(2,1)} %bitcast.2), calls=%async_computation | async-start | bytes 262144 | tf_op jit(solution)/shard_map/all_to_all | solution.py:14
  52.1 17.6 %copy-start.1 = (s32[8,4096]{1,0:T(8,128)S(1)}, s32[8,4096]{1,0:T(8,128)}, u32[]{:S(2)}) copy-start(s32[8,4096]{1,0:T(8,128)} %param.11) | copy-start | bytes 393220
  52.1 17.7 %copy-start.2 = (s32[8,4096]{1,0:T(8,128)S(1)}, s32[8,4096]{1,0:T(8,128)}, u32[]{:S(2)}) copy-start(s32[8,4096]{1,0:T(8,128)} %param.12) | copy-start | bytes 393220
  52.1 378.1 %all-to-all-start.1 = ((bf16[256,128,128]{2,1,0:T(8,128)(2,1)}), bf16[256,128,128]{2,1,0:T(8,128)(2,1)}, u32[]{:S(2)}, u32[]{:S(2)}) async-start(bf16[256,128,128]{2,1,0:T(8,128)(2,1)} %copy.14), calls=%async_computation.1 | async-start | bytes 16777216 | tf_op jit(solution)/shard_map/all_to_all | solution.py:28
  69.7 1021.6 %reduce-scatter.2.cloned.1.call-start = ((), (), s32[]{:S(2)}) async-start(), calls=%async_computation.3 | async-start | bytes 2162688 | tf_op jit(solution)/shard_map/reduce_scatter | solution.py:32
Sparse Core Ops, SparseCore 0:
  986.4 104.8 reduce-scatter.1
where the time goes:
time: 1110 us; the launch traced here: 1100 us
  local copies, waits for them, and re-layouts  560 us (50%)
  waiting for transfers between devices  470 us (42%)
  starting transfers between devices  25.2 us (2%)
  matrix products  15.5 us (1%)
  other arithmetic  14.9 us (1%)
  between operations  13.5 us (1%)
    gather x1, local copies, waits for them, and re-layouts, take_rows(): return jnp.take(table, picks, axis=0)  530 us
    all_to_all x1, waiting for transfers between devices, body(): lax.all_to_all(mixed, 'beta', split_axis=0, concat_axis=2, tiled=True)  360 us
    reduce_scatter x1, waiting for transfers between devices, body(): lax.psum_scatter(terms, 'beta', scatter_dimension=1, tiled=True)  105 us
  transfers between devices with their start and end apart: 3, of which 3 were waited for; matrix products, arithmetic and copies ran while one was open for 0% of the time, Pallas kernels for 0%

commit v1 on v0

v1 whole, which is shorter than its diff:
```python
import functools

import jax
import jax.numpy as jnp
from jax import lax
from jax.experimental import pallas as pl
from jax.experimental.pallas import tpu as pltpu
from jax.sharding import PartitionSpec as P

MESH = pl.DeviceIdType.MESH
BF16, F32, I32 = jnp.bfloat16, jnp.float32, jnp.int32
BLK = 128
NP = 8
HALF = 64
UNIT = 4
LEAD = 8


def kernel(
    n_alpha, n_z,
    coeffs, send_rows, a_source, a_sign, b_source, b_sign, integrals,
    out,
    picked, received, table, src_t, sgn_t, v16, w_raw, w_out, w_full, w_t, big, idx_v, idx_s,
    rs_in, rs_out, sib_in, sib_out,
    pick_send, pick_recv, ring_send, ring_recv, half_send, half_recv, w_send, w_recv,
    rs_send, rs_recv, sib_send, sib_recv, idx_sem,
):
    a = lax.axis_index("alpha")
    b = lax.axis_index("beta")
    z, core = b // 2, b % 2
    cap = send_rows.shape[1]
    slots = n_alpha * cap
    n_pairs = integrals.shape[0]
    cols = b_source.shape[1]
    steps = n_z // 2
    first = 4 if steps >= 4 else 2
    units = HALF // UNIT
    units_pre = units - 4 * (first - 2)

    up = lax.rem(z + 1, n_z) * 2 + core
    down = lax.rem(z + n_z - 1, n_z) * 2 + core
    other = z * 2 + 1 - core

    barrier = pltpu.get_barrier_semaphore()
    for o in range(1, n_alpha):
        pl.semaphore_signal(barrier, inc=1, device_id=(lax.rem(a + o, n_alpha), b), device_id_type=MESH)
    for peer in (up, down, other):
        pl.semaphore_signal(barrier, inc=1, device_id=(a, peer), device_id_type=MESH)

    per = BLK // cap
    row_ids = lax.broadcasted_iota(I32, (BLK, BLK), 0)
    local = coeffs[...]
    for g in range(slots // BLK):
        line = jnp.concatenate([send_rows[g * per + k : g * per + k + 1, :] for k in range(per)], axis=1)
        hot = jnp.where(row_ids == line, 1.0, 0.0).T.astype(BF16)
        picked[g * BLK : (g + 1) * BLK, :] = jnp.dot(hot, local, preferred_element_type=F32).astype(BF16)
    pl.semaphore_wait(barrier, n_alpha - 1 + 3)

    def pick_copy(to, frm):
        return pltpu.make_async_remote_copy(
            src_ref=picked.at[pl.ds(pl.multiple_of(to * cap, cap), cap), :],
            dst_ref=received.at[pl.ds(pl.multiple_of(frm * cap, cap), cap), :],
            send_sem=pick_send.at[to], recv_sem=pick_recv.at[frm],
            device_id=(to, b), device_id_type=MESH)

    @pl.loop(1, n_alpha)
    def _(o):
        pick_copy(lax.rem(a + o, n_alpha), a).start()

    mine = pl.ds(pl.multiple_of(a * cap, cap), cap)
    received[mine, :] = picked[mine, :]

    src_t[...] = a_source[...].astype(F32).T
    sgn_t[...] = a_sign[...].astype(F32).T
    r16 = lax.broadcasted_iota(I32, (2 * NP, n_pairs), 0)
    c16 = lax.broadcasted_iota(I32, (2 * NP, n_pairs), 1)
    want = jnp.where(r16 < NP, b * NP + r16, other * NP + r16 - NP)
    v16[...] = jnp.dot(
        jnp.where(c16 == want, 1.0, 0.0).astype(BF16), integrals[...], preferred_element_type=F32).astype(BF16)
    pair_at = lax.broadcasted_iota(I32, (NP, BLK), 0) * (2 * cols) + LEAD
    pair_at = pair_at - lax.rem(lax.broadcasted_iota(I32, (NP, BLK), 1), 8)
    for c in range(cols // BLK):
        cut = slice(c * BLK, (c + 1) * BLK)
        idx_v[c] = b_source[:, cut] + jnp.where(b_sign[:, cut] < 0, cols, 0) + pair_at

    slot_ids = lax.broadcasted_iota(I32, (slots, n_pairs), 0).astype(F32)

    def weight_unit(unit):
        for k in range(UNIT):
            at = unit * UNIT + k
            line = pl.ds(core * HALF + at, 1)
            hot = jnp.where(slot_ids == src_t[line, :], sgn_t[line, :], 0.0).astype(BF16)
            w_raw[at] = lax.dot_general(v16[...], hot, (((1,), (1,)), ((), ())), preferred_element_type=F32)

    @pl.loop(0, units_pre)
    def _(unit):
        weight_unit(unit)

    @pl.loop(1, n_alpha)
    def _(o):
        pick_copy(a, lax.rem(a + o, n_alpha)).wait_recv()

    table[b] = received[...].astype(F32).T.astype(BF16)

    def half_rows(h):
        return pl.ds(pl.multiple_of(h * HALF, HALF), HALF)

    def ring_copy(m, origin, d, h):
        ref = table.at[origin * 2 + core, half_rows(h), :]
        return pltpu.make_async_remote_copy(
            src_ref=ref, dst_ref=ref, send_sem=ring_send.at[m], recv_sem=ring_recv.at[m],
            device_id=(a, jnp.where(d == 0, up, down)), device_id_type=MESH)

    def half_copy(n, h, origin, who):
        ref = table.at[origin * 2 + who, half_rows(h), :]
        return pltpu.make_async_remote_copy(
            src_ref=ref, dst_ref=ref, send_sem=half_send.at[n * 2 + h], recv_sem=half_recv.at[n * 2 + h],
            device_id=(a, other), device_id_type=MESH)

    for h in range(2):
        for d in range(2):
            ring_copy(h * 2 + d, z, d, h).start()
    for h in range(2):
        half_copy(0, h, z, core).start()

    def w_copy():
        return pltpu.make_async_remote_copy(
            src_ref=w_out, dst_ref=w_full.at[:, half_rows(core), :],
            send_sem=w_send, recv_sem=w_recv, device_id=(a, other), device_id_type=MESH)

    def w_wait():
        return pltpu.make_async_remote_copy(
            src_ref=w_out, dst_ref=w_full.at[:, half_rows(1 - core), :],
            send_sem=w_send, recv_sem=w_recv, device_id=(a, other), device_id_type=MESH)

    def origin_of(n):
        s = (n + 1) // 2
        return lax.rem(jnp.where(n % 2 == 1, z - s, z + s) + n_z, n_z)

    def mix(n):
        origin = origin_of(n)
        for h in range(2):
            half_copy(n, h, origin, 1 - core).wait_recv()
        rows = table[pl.ds(origin * 2, 2)].reshape(2 * BLK, slots)
        for p in range(0, NP, 2):
            r = jnp.dot(rows, w_t[:, p * BLK : (p + 2) * BLK], preferred_element_type=F32)
            for k in range(2):
                at = LEAD + (p + k) * 2 * cols + origin * (2 * BLK)
                x = r[:, k * BLK : (k + 1) * BLK]
                big[pl.ds(pl.multiple_of(at, 8), 2 * BLK), :] = x
                big[pl.ds(pl.multiple_of(at + cols, 8), 2 * BLK), :] = -x

    def target(s):
        return jnp.maximum(jnp.minimum(4 * (s - first) + 3, 2 * s - 1), 0)

    @pl.loop(0, 4 * steps)
    def _(m):
        s, d, h = m // 4 + 1, m % 2, (m % 4) // 2
        origin = lax.rem(jnp.where(d == 0, z - s, z + s) + n_z, n_z)
        exists = jnp.logical_or(s < steps, d == h)
        onward = jnp.logical_or(s + 1 < steps, jnp.logical_and(s + 1 == steps, d == h))

        @pl.when(exists)
        def _():
            ring_copy(m, origin, d, h).wait_recv()

        @pl.when(onward)
        def _():
            ring_copy(m + 4, origin, d, h).start()

        @pl.when(exists)
        def _():
            half_copy(jnp.minimum(2 * s - 1 + d, n_z - 1), h, origin, core).start()

        if first > 2:
            @pl.when(m < 4 * (first - 2))
            def _():
                weight_unit(units_pre + m)

        @pl.when(m == 4 * (first - 2))
        def _():
            for p in range(NP):
                w_out[p] = w_raw[:, NP + p, :].astype(BF16)
            w_copy().start()
            for p in range(NP):
                w_full[p, half_rows(core), :] = w_raw[:, p, :].astype(BF16)

        @pl.when(m == 4 * (first - 1) - 1)
        def _():
            w_wait().wait_recv()
            for p in range(NP):
                w_t[:, p * BLK : (p + 1) * BLK] = w_full[p].astype(F32).T.astype(BF16)

        low, high = target(s - 1), target(s)
        k = m % 4

        @pl.loop(low + ((high - low) * k) // 4, low + ((high - low) * (k + 1)) // 4)
        def _(n):
            mix(n)

    def owner_of(i):
        t = i // 2
        away = jnp.where(i == n_z - 1, 0, jnp.where(i % 2 == 0, steps - t, t + 1 - steps))
        return lax.rem(z + away + n_z, n_z)

    def idx_copy(i, which):
        chunk = owner_of(i) * 2 + jnp.where(which == 0, 1 - core, core)
        return pltpu.make_async_copy(idx_v.at[chunk], idx_s.at[which], idx_sem.at[which])

    for which in range(2):
        idx_copy(0, which).start()

    @pl.loop(target(steps), n_z)
    def _(n):
        mix(n)

    sub = lax.broadcasted_iota(I32, (8, BLK), 0)

    def gather(which, dst):
        for u in range(BLK // 8):
            total = None
            for k in range(8):
                acc = None
                for p in range(NP):
                    v = big[pl.ds(idx_s[which, p, u * 8 + k], 8), :]
                    acc = v if acc is None else acc + v
                total = acc if total is None else jnp.where(sub == k, acc, total)
            dst[u * 8 : (u + 1) * 8, :] = total

    def sib_copy(i):
        return pltpu.make_async_remote_copy(
            src_ref=sib_out.at[i], dst_ref=sib_in.at[i], send_sem=sib_send.at[i], recv_sem=sib_recv.at[i],
            device_id=(a, other), device_id_type=MESH)

    def rs_copy(i):
        return pltpu.make_async_remote_copy(
            src_ref=rs_out.at[i], dst_ref=rs_in.at[i], send_sem=rs_send.at[i], recv_sem=rs_recv.at[i],
            device_id=(a, jnp.where(i % 2 == 0, up, down)), device_id_type=MESH)

    def pass_on(i):
        sib_copy(i).wait_recv()
        rs_out[i] = rs_out[i] + sib_in[i]

        @pl.when(i >= 2)
        def _():
            rs_copy(i - 2).wait_recv()
            rs_out[i] = rs_out[i] + rs_in[i - 2]

        rs_copy(i).start()

    @pl.loop(0, n_z)
    def _(i):
        idx_copy(i, 0).wait()
        gather(0, sib_out.at[i])
        sib_copy(i).start()

        @pl.when(i + 1 < n_z)
        def _():
            idx_copy(i + 1, 0).start()

        @pl.when(i > 0)
        def _():
            pass_on(i - 1)

        idx_copy(i, 1).wait()
        gather(1, rs_out.at[i])

        @pl.when(i + 1 < n_z)
        def _():
            idx_copy(i + 1, 1).start()

    last = n_z - 1
    sib_copy(last).wait_recv()
    rs_copy(last - 2).wait_recv()
    rs_copy(last - 1).wait_recv()
    total = (rs_out[last] + sib_in[last]) + (rs_in[last - 2] + rs_in[last - 1])
    out[...] = total.T.astype(BF16)

    @pl.loop(1, n_alpha)
    def _(o):
        pick_copy(lax.rem(a + o, n_alpha), a).wait_send()

    @pl.loop(0, 4 * steps)
    def _(m):
        s, d, h = m // 4 + 1, m % 2, (m % 4) // 2

        @pl.when(jnp.logical_or(s < steps, d == h))
        def _():
            ring_copy(m, z, d, h).wait_send()

    @pl.loop(0, 2 * n_z)
    def _(j):
        half_copy(j // 2, j % 2, z, core).wait_send()

    w_copy().wait_send()

    @pl.loop(0, n_z)
    def _(i):
        sib_copy(i).wait_send()

        @pl.when(i < n_z - 1)
        def _():
            rs_copy(i).wait_send()


def body(n_alpha, n_z, coeffs, send_rows, a_source, a_sign, b_source, b_sign, integrals):
    cap = send_rows.shape[1]
    slots = n_alpha * cap
    n_pairs = integrals.shape[0]
    cols = b_source.shape[1]
    V, DMA = pltpu.VMEM, pltpu.SemaphoreType.DMA
    blocks = 2 * n_z
    scratch = [
        V((slots, BLK), BF16), V((slots, BLK), BF16), V((blocks, BLK, slots), BF16),
        V((BLK, n_pairs), F32), V((BLK, n_pairs), F32), V((2 * NP, n_pairs), BF16),
        V((HALF, 2 * NP, slots), F32), V((NP, HALF, slots), BF16), V((NP, BLK, slots), BF16),
        V((slots, NP * BLK), BF16), V((NP * 2 * cols + 2 * LEAD, BLK), F32),
        V((cols // BLK, NP, BLK), I32), pltpu.SMEM((2, NP, BLK), I32),
        V((n_z, BLK, BLK), F32), V((n_z, BLK, BLK), F32), V((n_z, BLK, BLK), F32), V((n_z, BLK, BLK), F32),
        DMA((n_alpha,)), DMA((n_alpha,)), DMA((2 * n_z,)), DMA((2 * n_z,)), DMA((2 * n_z,)), DMA((2 * n_z,)),
        DMA, DMA, DMA((n_z,)), DMA((n_z,)), DMA((n_z,)), DMA((n_z,)), DMA((2,)),
    ]
    return pl.pallas_call(
        functools.partial(kernel, n_alpha, n_z),
        out_shape=jax.ShapeDtypeStruct((BLK, BLK), BF16),
        in_specs=[pl.BlockSpec(memory_space=V)] * 7,
        out_specs=pl.BlockSpec(memory_space=V),
        scratch_shapes=scratch,
        compiler_params=pltpu.CompilerParams(
            collective_id=0, has_side_effects=True, vmem_limit_bytes=60 * 2**20),
    )(coeffs, send_rows, a_source, a_sign, b_source, b_sign, integrals)


def solution(mesh):
    in_specs = (
        P("alpha", "beta"), P("alpha", None), P(None, "alpha"), P(None, "alpha"),
        P("beta", None), P("beta", None), P(),
    )
    run = functools.partial(body, mesh.shape["alpha"], mesh.shape["beta"] // 2)
    return jax.shard_map(run, mesh=mesh, in_specs=in_specs, out_specs=P("alpha", "beta"), check_vma=False)
```

time: 1110 us -> 89.6 us (0.08)
  local copies, waits for them, and re-layouts: 560 us -> 1.38 us
  waiting for transfers between devices: 470 us -> 0 us
  Pallas kernels: 0 us -> 87 us
  starting transfers between devices: 25.2 us -> 0 us
  matrix products: 15.5 us -> 0 us
  other arithmetic: 14.9 us -> 0 us
  between operations: 13.5 us -> 0.01 us
    gather x2 -> x0, local copies, waits for them, and re-layouts: 532 us -> none  [the longest x1 530 us: take_rows(): return jnp.take(table, picks, axis=0)]
    all_to_all x2 -> x0, waiting for transfers between devices: 365 us -> none  [the longest x1 360 us: body(): lax.all_to_all(mixed, 'beta', split_axis=0, concat_axis=2, tiled=True)]
    reduce_scatter x1 -> x0, waiting for transfers between devices: 105 us -> none  [body(): lax.psum_scatter(terms, 'beta', scatter_dimension=1, tiled=True)]
    pallas_call x0 -> x1, Pallas kernels: none -> 87 us  [body(): pl.pallas_call(functools.partial(kernel, n_alpha, n_z), out_shape=jax.Sha...]
    all_to_all x2 -> x0, starting transfers between devices: 25.1 us -> none  [the longest x1 17.5 us: body(): lax.all_to_all(mixed, 'beta', split_axis=0, concat_axis=2, tiled=True)]
    dot_general x1 -> x0, matrix products: 15.5 us -> none  [body(): jnp.einsum('pq,qrc->prc', integrals, excited, preferred_element_type=jnp....]
    unnamed x3 -> x0, other arithmetic: 12.6 us -> none
    convert_element_type x1 -> x0, local copies, waits for them, and re-layouts: 12.4 us -> none  [body(): mixed = jnp.einsum('pq,qrc->prc', integrals, excited, preferred_element_t...]
  transfers between devices with their start and end apart: 3 -> 0, of which waited for: 3 -> 0; matrix products, arithmetic and copies ran while one was open for 0% -> 0% of each run, Pallas kernels for 0% -> 0%
where the time goes in v1:
time: 89.6 us; the launch traced here: 88.4 us
  Pallas kernels  87 us (97%)
  local copies, waits for them, and re-layouts  1.38 us (2%)
    pallas_call x1, Pallas kernels, body(): pl.pallas_call(functools.partial(kernel, n_alpha, n_z), out_shape=jax.Sha...  87 us

profile of v1, /device:TPU:1, one launch (start us, length us, event | category | flops | bytes accessed | tf_op | source)
XLA Modules:
  0.0 88.4 jit_solution(9200966208898071159)
XLA Ops:
  0.0 87.0 %shard_map.73 = bf16[128,128]{1,0:T(8,128)(2,1)} custom-call(bf16[128,128]{1,0:T(8,128)(2,1)} %coeffs.1, s32[16,32]{1,0:T(8,128)} %send_rows.1, s32[256,128]{1,0:T(8,128)} %a_source.1, s32[256,128]{1,0:T(8,128)} %a_sign.1, s32[8,4096]{1,0:T(8,128)} %b_source.1, s32[8,4096]{1,0:T(8,128)} %b_sign.1, bf16[256,256]{1,0:T(8,128)(2,1)} %integrals.1), custom_call_target="tpu_custom_call" | custom-call | tf_op jit(solution)/shard_map/pallas_call | solution.py:323
  87.0 1.4 %copy.9 = bf16[128,128]{1,0:T(8,128)(2,1)} copy(bf16[128,128]{1,0:T(8,128)(2,1)} %shard_map.73) | data formatting | bytes 65536

commit v2 on v1

--- a/solution.py
+++ b/solution.py
@@ -12,8 +12,12 @@
 BLK = 128
 NP = 8
 HALF = 64
+PARTS = 4
+PART = BLK // PARTS
+ROUND = 2 * PARTS
 UNIT = 4
 LEAD = 8
+LAG = 5
 
 
 def kernel(
@@ -21,9 +25,9 @@
     coeffs, send_rows, a_source, a_sign, b_source, b_sign, integrals,
     out,
     picked, received, table, src_t, sgn_t, v16, w_raw, w_out, w_full, w_t, big, idx_v, idx_s,
-    rs_in, rs_out, sib_in, sib_out,
+    rs_in, rs_out, mate_in, mate_out, terms, sib_in, sib_out,
     pick_send, pick_recv, ring_send, ring_recv, half_send, half_recv, w_send, w_recv,
-    rs_send, rs_recv, sib_send, sib_recv, idx_sem,
+    rs_send, rs_recv, mate_send, mate_recv, sib_send, sib_recv, idx_sem,
 ):
     a = lax.axis_index("alpha")
     b = lax.axis_index("beta")
@@ -35,7 +39,7 @@
     steps = n_z // 2
     first = 4 if steps >= 4 else 2
     units = HALF // UNIT
-    units_pre = units - 4 * (first - 2)
+    units_pre = units - ROUND // 2 * (first - 2)
 
     up = lax.rem(z + 1, n_z) * 2 + core
     down = lax.rem(z + n_z - 1, n_z) * 2 + core
@@ -106,7 +110,7 @@
         return pl.ds(pl.multiple_of(h * HALF, HALF), HALF)
 
     def ring_copy(m, origin, d, h):
-        ref = table.at[origin * 2 + core, half_rows(h), :]
+        ref = table.at[origin * 2 + core, pl.ds(pl.multiple_of(h * PART, PART), PART), :]
         return pltpu.make_async_remote_copy(
             src_ref=ref, dst_ref=ref, send_sem=ring_send.at[m], recv_sem=ring_recv.at[m],
             device_id=(a, jnp.where(d == 0, up, down)), device_id_type=MESH)
@@ -117,7 +121,7 @@
             src_ref=ref, dst_ref=ref, send_sem=half_send.at[n * 2 + h], recv_sem=half_recv.at[n * 2 + h],
             device_id=(a, other), device_id_type=MESH)
 
-    for h in range(2):
+    for h in range(PARTS):
         for d in range(2):
             ring_copy(h * 2 + d, z, d, h).start()
     for h in range(2):
@@ -153,12 +157,13 @@
     def target(s):
         return jnp.maximum(jnp.minimum(4 * (s - first) + 3, 2 * s - 1), 0)
 
-    @pl.loop(0, 4 * steps)
+    @pl.loop(0, ROUND * steps)
     def _(m):
-        s, d, h = m // 4 + 1, m % 2, (m % 4) // 2
+        s, d, h = m // ROUND + 1, m % 2, (m % ROUND) // 2
         origin = lax.rem(jnp.where(d == 0, z - s, z + s) + n_z, n_z)
-        exists = jnp.logical_or(s < steps, d == h)
-        onward = jnp.logical_or(s + 1 < steps, jnp.logical_and(s + 1 == steps, d == h))
+        its_way = d == h // (PARTS // 2)
+        exists = jnp.logical_or(s < steps, its_way)
+        onward = jnp.logical_or(s + 1 < steps, jnp.logical_and(s + 1 == steps, its_way))
 
         @pl.when(exists)
         def _():
@@ -166,18 +171,18 @@
 
         @pl.when(onward)
         def _():
-            ring_copy(m + 4, origin, d, h).start()
-
-        @pl.when(exists)
-        def _():
-            half_copy(jnp.minimum(2 * s - 1 + d, n_z - 1), h, origin, core).start()
+            ring_copy(m + ROUND, origin, d, h).start()
+
+        @pl.when(jnp.logical_and(exists, h % 2 == 1))
+        def _():
+            half_copy(jnp.minimum(2 * s - 1 + d, n_z - 1), h // 2, origin, core).start()
 
         if first > 2:
-            @pl.when(m < 4 * (first - 2))
+            @pl.when(jnp.logical_and(m < ROUND * (first - 2), m % 2 == 0))
             def _():
-                weight_unit(units_pre + m)
-
-        @pl.when(m == 4 * (first - 2))
+                weight_unit(units_pre + m // 2)
+
+        @pl.when(m == ROUND * (first - 2))
         def _():
             for p in range(NP):
                 w_out[p] = w_raw[:, NP + p, :].astype(BF16)
@@ -185,23 +190,25 @@
             for p in range(NP):
                 w_full[p, half_rows(core), :] = w_raw[:, p, :].astype(BF16)
 
-        @pl.when(m == 4 * (first - 1) - 1)
+        @pl.when(m == ROUND * (first - 1) - 1)
         def _():
             w_wait().wait_recv()
             for p in range(NP):
                 w_t[:, p * BLK : (p + 1) * BLK] = w_full[p].astype(F32).T.astype(BF16)
 
         low, high = target(s - 1), target(s)
-        k = m % 4
-
-        @pl.loop(low + ((high - low) * k) // 4, low + ((high - low) * (k + 1)) // 4)
+        k = m % ROUND
+
+        @pl.loop(low + ((high - low) * k) // ROUND, low + ((high - low) * (k + 1)) // ROUND)
         def _(n):
             mix(n)
 
+    side = jnp.where(z % 2 == 1, 1, -1)
+    mate = lax.rem(z - side + n_z, n_z)
+
     def owner_of(i):
-        t = i // 2
-        away = jnp.where(i == n_z - 1, 0, jnp.where(i % 2 == 0, steps - t, t + 1 - steps))
-        return lax.rem(z + away + n_z, n_z)
+        far = steps - 1 - i // 2
+        return lax.rem(jnp.where(i % 2 == 1, z + side * far, mate - side * far) + n_z, n_z)
 
     def idx_copy(i, which):
         chunk = owner_of(i) * 2 + jnp.where(which == 0, 1 - core, core)
@@ -232,21 +239,29 @@
             src_ref=sib_out.at[i], dst_ref=sib_in.at[i], send_sem=sib_send.at[i], recv_sem=sib_recv.at[i],
             device_id=(a, other), device_id_type=MESH)
 
-    def rs_copy(i):
-        return pltpu.make_async_remote_copy(
-            src_ref=rs_out.at[i], dst_ref=rs_in.at[i], send_sem=rs_send.at[i], recv_sem=rs_recv.at[i],
-            device_id=(a, jnp.where(i % 2 == 0, up, down)), device_id_type=MESH)
-
-    def pass_on(i):
+    def mate_copy(t):
+        return pltpu.make_async_remote_copy(
+            src_ref=mate_out.at[t], dst_ref=mate_in.at[t], send_sem=mate_send.at[t], recv_sem=mate_recv.at[t],
+            device_id=(a, mate * 2 + core), device_id_type=MESH)
+
+    def rs_copy(t):
+        return pltpu.make_async_remote_copy(
+            src_ref=rs_out.at[t], dst_ref=rs_in.at[t], send_sem=rs_send.at[t], recv_sem=rs_recv.at[t],
+            device_id=(a, owner_of(2 * t + 1) * 2 + core), device_id_type=MESH)
+
+    def pass_on(t):
+        mate_copy(t).wait_recv()
+        rs_out[t] = (terms[2 * t + 1] + mate_in[t].astype(F32)).astype(BF16)
+        rs_copy(t).start()
+
+    def chip_sum(i):
         sib_copy(i).wait_recv()
-        rs_out[i] = rs_out[i] + sib_in[i]
-
-        @pl.when(i >= 2)
-        def _():
-            rs_copy(i - 2).wait_recv()
-            rs_out[i] = rs_out[i] + rs_in[i - 2]
-
-        rs_copy(i).start()
+        terms[i] = terms[i] + sib_in[i]
+
+        @pl.when(i % 2 == 0)
+        def _():
+            mate_out[i // 2] = terms[i].astype(BF16)
+            mate_copy(i // 2).start()
 
     @pl.loop(0, n_z)
     def _(i):
@@ -260,31 +275,39 @@
 
         @pl.when(i > 0)
         def _():
-            pass_on(i - 1)
+            chip_sum(i - 1)
+
+        @pl.when(jnp.logical_and(i % 2 == 1, i >= LAG))
+        def _():
+            pass_on((i - LAG) // 2)
 
         idx_copy(i, 1).wait()
-        gather(1, rs_out.at[i])
+        gather(1, terms.at[i])
 
         @pl.when(i + 1 < n_z)
         def _():
             idx_copy(i + 1, 1).start()
 
     last = n_z - 1
-    sib_copy(last).wait_recv()
-    rs_copy(last - 2).wait_recv()
-    rs_copy(last - 1).wait_recv()
-    total = (rs_out[last] + sib_in[last]) + (rs_in[last - 2] + rs_in[last - 1])
+    for t in range((last - LAG) // 2 + 1, steps - 1):
+        pass_on(t)
+    chip_sum(last)
+    mate_copy(steps - 1).wait_recv()
+    total = terms[last] + mate_in[steps - 1].astype(F32)
+    for t in range(steps - 1):
+        rs_copy(t).wait_recv()
+        total = total + rs_in[t].astype(F32)
     out[...] = total.T.astype(BF16)
 
     @pl.loop(1, n_alpha)
     def _(o):
         pick_copy(lax.rem(a + o, n_alpha), a).wait_send()
 
-    @pl.loop(0, 4 * steps)
+    @pl.loop(0, ROUND * steps)
     def _(m):
-        s, d, h = m // 4 + 1, m % 2, (m % 4) // 2
-
-        @pl.when(jnp.logical_or(s < steps, d == h))
+        s, d, h = m // ROUND + 1, m % 2, (m % ROUND) // 2
+
+        @pl.when(jnp.logical_or(s < steps, d == h // (PARTS // 2)))
         def _():
             ring_copy(m, z, d, h).wait_send()
 
@@ -298,9 +321,13 @@
     def _(i):
         sib_copy(i).wait_send()
 
-        @pl.when(i < n_z - 1)
-        def _():
-            rs_copy(i).wait_send()
+    @pl.loop(0, steps)
+    def _(t):
+        mate_copy(t).wait_send()
+
+        @pl.when(t < steps - 1)
+        def _():
+            rs_copy(t).wait_send()
 
 
 def body(n_alpha, n_z, coeffs, send_rows, a_source, a_sign, b_source, b_sign, integrals):
@@ -309,16 +336,18 @@
     n_pairs = integrals.shape[0]
     cols = b_source.shape[1]
     V, DMA = pltpu.VMEM, pltpu.SemaphoreType.DMA
-    blocks = 2 * n_z
+    blocks, half = 2 * n_z, n_z // 2
     scratch = [
         V((slots, BLK), BF16), V((slots, BLK), BF16), V((blocks, BLK, slots), BF16),
         V((BLK, n_pairs), F32), V((BLK, n_pairs), F32), V((2 * NP, n_pairs), BF16),
         V((HALF, 2 * NP, slots), F32), V((NP, HALF, slots), BF16), V((NP, BLK, slots), BF16),
         V((slots, NP * BLK), BF16), V((NP * 2 * cols + 2 * LEAD, BLK), F32),
         V((cols // BLK, NP, BLK), I32), pltpu.SMEM((2, NP, BLK), I32),
-        V((n_z, BLK, BLK), F32), V((n_z, BLK, BLK), F32), V((n_z, BLK, BLK), F32), V((n_z, BLK, BLK), F32),
-        DMA((n_alpha,)), DMA((n_alpha,)), DMA((2 * n_z,)), DMA((2 * n_z,)), DMA((2 * n_z,)), DMA((2 * n_z,)),
-        DMA, DMA, DMA((n_z,)), DMA((n_z,)), DMA((n_z,)), DMA((n_z,)), DMA((2,)),
+        V((half, BLK, BLK), BF16), V((half, BLK, BLK), BF16), V((half, BLK, BLK), BF16), V((half, BLK, BLK), BF16),
+        V((n_z, BLK, BLK), F32), V((n_z, BLK, BLK), F32), V((n_z, BLK, BLK), F32),
+        DMA((n_alpha,)), DMA((n_alpha,)), DMA((PARTS * n_z,)), DMA((PARTS * n_z,)),
+        DMA((2 * n_z,)), DMA((2 * n_z,)),
+        DMA, DMA, DMA((half,)), DMA((half,)), DMA((half,)), DMA((half,)), DMA((n_z,)), DMA((n_z,)), DMA((2,)),
     ]
     return pl.pallas_call(
         functools.partial(kernel, n_alpha, n_z),

time: 89.6 us -> 83.3 us (0.930); the launches traced: 88.4 us -> 83.1 us
  Pallas kernels: 87 us -> 81.7 us
    pallas_call x1, Pallas kernels: 87 us -> 81.7 us  [body(): pl.pallas_call(functools.partial(kernel, n_alpha, n_z), out_shape=jax.Sha...]
where the time goes in v2:
time: 83.3 us; the launch traced here: 83.1 us
  Pallas kernels  81.7 us (98%)
  local copies, waits for them, and re-layouts  1.38 us (2%)
    pallas_call x1, Pallas kernels, body(): pl.pallas_call(functools.partial(kernel, n_alpha, n_z), out_shape=jax.Sha...  81.7 us

profile of v2, /device:TPU:1, one launch (start us, length us, event | category | flops | bytes accessed | tf_op | source)
XLA Modules:
  0.0 83.1 jit_solution(13879500965764108674)
XLA Ops:
  0.0 81.7 %shard_map.73 = bf16[128,128]{1,0:T(8,128)(2,1)} custom-call(bf16[128,128]{1,0:T(8,128)(2,1)} %coeffs.1, s32[16,32]{1,0:T(8,128)} %send_rows.1, s32[256,128]{1,0:T(8,128)} %a_source.1, s32[256,128]{1,0:T(8,128)} %a_sign.1, s32[8,4096]{1,0:T(8,128)} %b_source.1, s32[8,4096]{1,0:T(8,128)} %b_sign.1, bf16[256,256]{1,0:T(8,128)(2,1)} %integrals.1), custom_call_target="tpu_custom_call" | custom-call | tf_op jit(solution)/shard_map/pallas_call | solution.py:352
  81.7 1.4 %copy.9 = bf16[128,128]{1,0:T(8,128)(2,1)} copy(bf16[128,128]{1,0:T(8,128)(2,1)} %shard_map.73) | data formatting | bytes 65536

commit v3 on v2

--- a/solution.py
+++ b/solution.py
@@ -18,15 +18,18 @@
 UNIT = 4
 LEAD = 8
 LAG = 5
+HOPS = 5
+FAR = 6
+GROUPS = ((0, 2), (2, 3))
 
 
 def kernel(
     n_alpha, n_z,
     coeffs, send_rows, a_source, a_sign, b_source, b_sign, integrals,
     out,
-    picked, received, table, src_t, sgn_t, v16, w_raw, w_out, w_full, w_t, big, idx_v, idx_s,
+    picked, received, hot, raw, far_picked, far_received, table, src_t, sgn_t, v16, w_raw, w_out, w_full, w_t, big, idx_v, idx_s,
     rs_in, rs_out, mate_in, mate_out, terms, sib_in, sib_out,
-    pick_send, pick_recv, ring_send, ring_recv, half_send, half_recv, w_send, w_recv,
+    pick_send, pick_recv, raw_send, raw_recv, far_send, far_recv, ring_send, ring_recv, half_send, half_recv, w_send, w_recv,
     rs_send, rs_recv, mate_send, mate_recv, sib_send, sib_recv, idx_sem,
 ):
     a = lax.axis_index("alpha")
@@ -37,18 +40,18 @@
     n_pairs = integrals.shape[0]
     cols = b_source.shape[1]
     steps = n_z // 2
-    first = 4 if steps >= 4 else 2
     units = HALF // UNIT
-    units_pre = units - ROUND // 2 * (first - 2)
-
-    up = lax.rem(z + 1, n_z) * 2 + core
-    down = lax.rem(z + n_z - 1, n_z) * 2 + core
+
+    def along(away):
+        return lax.rem(z + away + n_z, n_z) * 2 + core
+
+    up, down = along(1), along(-1)
     other = z * 2 + 1 - core
 
     barrier = pltpu.get_barrier_semaphore()
     for o in range(1, n_alpha):
         pl.semaphore_signal(barrier, inc=1, device_id=(lax.rem(a + o, n_alpha), b), device_id_type=MESH)
-    for peer in (up, down, other):
+    for peer in (along(FAR), along(-FAR), along(-2), up, down, other):
         pl.semaphore_signal(barrier, inc=1, device_id=(a, peer), device_id_type=MESH)
 
     per = BLK // cap
@@ -56,23 +59,9 @@
     local = coeffs[...]
     for g in range(slots // BLK):
         line = jnp.concatenate([send_rows[g * per + k : g * per + k + 1, :] for k in range(per)], axis=1)
-        hot = jnp.where(row_ids == line, 1.0, 0.0).T.astype(BF16)
-        picked[g * BLK : (g + 1) * BLK, :] = jnp.dot(hot, local, preferred_element_type=F32).astype(BF16)
-    pl.semaphore_wait(barrier, n_alpha - 1 + 3)
-
-    def pick_copy(to, frm):
-        return pltpu.make_async_remote_copy(
-            src_ref=picked.at[pl.ds(pl.multiple_of(to * cap, cap), cap), :],
-            dst_ref=received.at[pl.ds(pl.multiple_of(frm * cap, cap), cap), :],
-            send_sem=pick_send.at[to], recv_sem=pick_recv.at[frm],
-            device_id=(to, b), device_id_type=MESH)
-
-    @pl.loop(1, n_alpha)
-    def _(o):
-        pick_copy(lax.rem(a + o, n_alpha), a).start()
-
-    mine = pl.ds(pl.multiple_of(a * cap, cap), cap)
-    received[mine, :] = picked[mine, :]
+        cut = slice(g * BLK, (g + 1) * BLK)
+        hot[cut, :] = jnp.where(row_ids == line, 1.0, 0.0).T.astype(BF16)
+        picked[cut, :] = jnp.dot(hot[cut, :], local, preferred_element_type=F32).astype(BF16)
 
     src_t[...] = a_source[...].astype(F32).T
     sgn_t[...] = a_sign[...].astype(F32).T
@@ -93,12 +82,65 @@
         for k in range(UNIT):
             at = unit * UNIT + k
             line = pl.ds(core * HALF + at, 1)
-            hot = jnp.where(slot_ids == src_t[line, :], sgn_t[line, :], 0.0).astype(BF16)
-            w_raw[at] = lax.dot_general(v16[...], hot, (((1,), (1,)), ((), ())), preferred_element_type=F32)
-
-    @pl.loop(0, units_pre)
+            pick = jnp.where(slot_ids == src_t[line, :], sgn_t[line, :], 0.0).astype(BF16)
+            w_raw[at] = lax.dot_general(v16[...], pick, (((1,), (1,)), ((), ())), preferred_element_type=F32)
+
+    @pl.loop(0, units // 2)
     def _(unit):
         weight_unit(unit)
+
+    pl.semaphore_wait(barrier, n_alpha - 1 + 6)
+
+    def raw_copy(j):
+        away = (FAR, -FAR, 1, 2, -1)[j]
+        return pltpu.make_async_remote_copy(
+            src_ref=(coeffs, coeffs, raw.at[0], raw.at[0], raw.at[1])[j], dst_ref=raw.at[j],
+            send_sem=raw_send.at[j], recv_sem=raw_recv.at[j], device_id=(a, along(away)), device_id_type=MESH)
+
+    for j in range(2):
+        raw_copy(j).start()
+
+    def pick_copy(to, frm):
+        return pltpu.make_async_remote_copy(
+            src_ref=picked.at[pl.ds(pl.multiple_of(to * cap, cap), cap), :],
+            dst_ref=received.at[pl.ds(pl.multiple_of(frm * cap, cap), cap), :],
+            send_sem=pick_send.at[to], recv_sem=pick_recv.at[frm],
+            device_id=(to, b), device_id_type=MESH)
+
+    @pl.loop(1, n_alpha)
+    def _(o):
+        pick_copy(lax.rem(a + o, n_alpha), a).start()
+
+    mine = pl.ds(pl.multiple_of(a * cap, cap), cap)
+    received[mine, :] = picked[mine, :]
+
+    def half_rows(h):
+        return pl.ds(pl.multiple_of(h * HALF, HALF), HALF)
+
+    def w_copy():
+        return pltpu.make_async_remote_copy(
+            src_ref=w_out, dst_ref=w_full.at[:, half_rows(core), :],
+            send_sem=w_send, recv_sem=w_recv, device_id=(a, other), device_id_type=MESH)
+
+    def w_wait():
+        return pltpu.make_async_remote_copy(
+            src_ref=w_out, dst_ref=w_full.at[:, half_rows(1 - core), :],
+            send_sem=w_send, recv_sem=w_recv, device_id=(a, other), device_id_type=MESH)
+
+    @pl.loop(units // 2, units)
+    def _(unit):
+        weight_unit(unit)
+
+    for p in range(NP):
+        w_out[p] = w_raw[:, NP + p, :].astype(BF16)
+    w_copy().start()
+    for p in range(NP):
+        w_full[p, half_rows(core), :] = w_raw[:, p, :].astype(BF16)
+
+    for j in range(2):
+        raw_copy(j).wait_recv()
+    for j in range(2, 5):
+        raw_copy(j).start()
 
     @pl.loop(1, n_alpha)
     def _(o):
@@ -106,8 +148,12 @@
 
     table[b] = received[...].astype(F32).T.astype(BF16)
 
-    def half_rows(h):
-        return pl.ds(pl.multiple_of(h * HALF, HALF), HALF)
+    def origin_of(n):
+        s = (n + 1) // 2
+        away = jnp.where(n % 2 == 1, -s, s)
+        for j, far in enumerate((-FAR, FAR, -FAR - 1, -FAR - 2, FAR + 1)):
+            away = jnp.where(n == 2 * HOPS + 1 + j, far, away)
+        return lax.rem(z + away + n_z, n_z)
 
     def ring_copy(m, origin, d, h):
         ref = table.at[origin * 2 + core, pl.ds(pl.multiple_of(h * PART, PART), PART), :]
@@ -127,21 +173,41 @@
     for h in range(2):
         half_copy(0, h, z, core).start()
 
-    def w_copy():
-        return pltpu.make_async_remote_copy(
-            src_ref=w_out, dst_ref=w_full.at[:, half_rows(core), :],
-            send_sem=w_send, recv_sem=w_recv, device_id=(a, other), device_id_type=MESH)
-
-    def w_wait():
-        return pltpu.make_async_remote_copy(
-            src_ref=w_out, dst_ref=w_full.at[:, half_rows(1 - core), :],
-            send_sem=w_send, recv_sem=w_recv, device_id=(a, other), device_id_type=MESH)
-
-    def origin_of(n):
-        s = (n + 1) // 2
-        return lax.rem(jnp.where(n % 2 == 1, z - s, z + s) + n_z, n_z)
-
-    def mix(n):
+    def far_copy(g, to, frm):
+        low, count = GROUPS[g]
+        return pltpu.make_async_remote_copy(
+            src_ref=far_picked.at[pl.ds(low, count), pl.ds(pl.multiple_of(to * cap, cap), cap), :],
+            dst_ref=far_received.at[pl.ds(low, count), pl.ds(pl.multiple_of(frm * cap, cap), cap), :],
+            send_sem=far_send.at[g * n_alpha + to], recv_sem=far_recv.at[g * n_alpha + frm],
+            device_id=(to, b), device_id_type=MESH)
+
+    def far_pick(g):
+        low, count = GROUPS[g]
+        for j in range(low, low + count):
+            far_picked[j] = jnp.dot(hot[...], raw[j], preferred_element_type=F32).astype(BF16)
+
+        @pl.loop(1, n_alpha)
+        def _(o):
+            far_copy(g, lax.rem(a + o, n_alpha), a).start()
+
+        for j in range(low, low + count):
+            far_received[j, mine, :] = far_picked[j, mine, :]
+
+    def far_wait(g):
+        @pl.loop(1, n_alpha)
+        def _(o):
+            far_copy(g, a, lax.rem(a + o, n_alpha)).wait_recv()
+
+    def far_turn(j):
+        n = 2 * HOPS + 1 + j
+        origin = origin_of(n)
+        table[origin * 2 + core] = far_received[j].astype(F32).T.astype(BF16)
+        for h in range(2):
+            half_copy(n, h, origin, core).start()
+
+    def mix(k):
+        n = jnp.where(k == 7, 11, jnp.where(k == 10, 12, jnp.where(k < 7, k, jnp.where(k < 10, k - 1, k - 2))))
+        n = jnp.where(k > 12, k, n)
         origin = origin_of(n)
         for h in range(2):
             half_copy(n, h, origin, 1 - core).wait_recv()
@@ -154,47 +220,33 @@
                 big[pl.ds(pl.multiple_of(at, 8), 2 * BLK), :] = x
                 big[pl.ds(pl.multiple_of(at + cols, 8), 2 * BLK), :] = -x
 
+    far_pick(0)
+    w_wait().wait_recv()
+    for p in range(NP):
+        w_t[:, p * BLK : (p + 1) * BLK] = w_full[p].astype(F32).T.astype(BF16)
+
     def target(s):
-        return jnp.maximum(jnp.minimum(4 * (s - first) + 3, 2 * s - 1), 0)
-
-    @pl.loop(0, ROUND * steps)
+        return jnp.maximum(jnp.maximum(2 * s - 1, 3 * s - 4), 0)
+
+    @pl.loop(0, ROUND * HOPS)
     def _(m):
         s, d, h = m // ROUND + 1, m % 2, (m % ROUND) // 2
         origin = lax.rem(jnp.where(d == 0, z - s, z + s) + n_z, n_z)
-        its_way = d == h // (PARTS // 2)
-        exists = jnp.logical_or(s < steps, its_way)
-        onward = jnp.logical_or(s + 1 < steps, jnp.logical_and(s + 1 == steps, its_way))
-
-        @pl.when(exists)
-        def _():
-            ring_copy(m, origin, d, h).wait_recv()
-
-        @pl.when(onward)
+        ring_copy(m, origin, d, h).wait_recv()
+
+        @pl.when(s < HOPS)
         def _():
             ring_copy(m + ROUND, origin, d, h).start()
 
-        @pl.when(jnp.logical_and(exists, h % 2 == 1))
-        def _():
-            half_copy(jnp.minimum(2 * s - 1 + d, n_z - 1), h // 2, origin, core).start()
-
-        if first > 2:
-            @pl.when(jnp.logical_and(m < ROUND * (first - 2), m % 2 == 0))
-            def _():
-                weight_unit(units_pre + m // 2)
-
-        @pl.when(m == ROUND * (first - 2))
-        def _():
-            for p in range(NP):
-                w_out[p] = w_raw[:, NP + p, :].astype(BF16)
-            w_copy().start()
-            for p in range(NP):
-                w_full[p, half_rows(core), :] = w_raw[:, p, :].astype(BF16)
-
-        @pl.when(m == ROUND * (first - 1) - 1)
-        def _():
-            w_wait().wait_recv()
-            for p in range(NP):
-                w_t[:, p * BLK : (p + 1) * BLK] = w_full[p].astype(F32).T.astype(BF16)
+        @pl.when(h % 2 == 1)
+        def _():
+            half_copy(2 * s - 1 + d, h // 2, origin, core).start()
+
+        @pl.when(m == ROUND - 1)
+        def _():
+            for j in range(2, 5):
+                raw_copy(j).wait_recv()
+            far_pick(1)
 
         low, high = target(s - 1), target(s)
         k = m % ROUND
@@ -203,6 +255,15 @@
         def _(n):
             mix(n)
 
+        @pl.when(m == 3 * ROUND - 1)
+        def _():
+            far_wait(0)
+            far_turn(0)
+
+        @pl.when(m == 4 * ROUND - 1)
+        def _():
+            far_turn(1)
+
     side = jnp.where(z % 2 == 1, 1, -1)
     mate = lax.rem(z - side + n_z, n_z)
 
@@ -217,7 +278,11 @@
     for which in range(2):
         idx_copy(0, which).start()
 
-    @pl.loop(target(steps), n_z)
+    far_wait(1)
+    for j in range(2, 5):
+        far_turn(j)
+
+    @pl.loop(3 * HOPS - 4, n_z)
     def _(n):
         mix(n)
 
@@ -291,6 +356,38 @@
     last = n_z - 1
     for t in range((last - LAG) // 2 + 1, steps - 1):
         pass_on(t)
+    @pl.loop(1, n_alpha)
+    def _(o):
+        pick_copy(lax.rem(a + o, n_alpha), a).wait_send()
+
+        for g in range(2):
+            far_copy(g, lax.rem(a + o, n_alpha), a).wait_send()
+
+    for j in range(5):
+        raw_copy(j).wait_send()
+
+    @pl.loop(0, ROUND * HOPS)
+    def _(m):
+        ring_copy(m, z, m % 2, (m % ROUND) // 2).wait_send()
+
+    @pl.loop(0, 2 * n_z)
+    def _(j):
+        half_copy(j // 2, j % 2, z, core).wait_send()
+
+    w_copy().wait_send()
+
+    @pl.loop(0, n_z)
+    def _(i):
+        sib_copy(i).wait_send()
+
+    @pl.loop(0, steps)
+    def _(t):
+        mate_copy(t).wait_send()
+
+        @pl.when(t < steps - 1)
+        def _():
+            rs_copy(t).wait_send()
+
     chip_sum(last)
     mate_copy(steps - 1).wait_recv()
     total = terms[last] + mate_in[steps - 1].astype(F32)
@@ -298,36 +395,6 @@
         rs_copy(t).wait_recv()
         total = total + rs_in[t].astype(F32)
     out[...] = total.T.astype(BF16)
-
-    @pl.loop(1, n_alpha)
-    def _(o):
-        pick_copy(lax.rem(a + o, n_alpha), a).wait_send()
-
-    @pl.loop(0, ROUND * steps)
-    def _(m):
-        s, d, h = m // ROUND + 1, m % 2, (m % ROUND) // 2
-
-        @pl.when(jnp.logical_or(s < steps, d == h // (PARTS // 2)))
-        def _():
-            ring_copy(m, z, d, h).wait_send()
-
-    @pl.loop(0, 2 * n_z)
-    def _(j):
-        half_copy(j // 2, j % 2, z, core).wait_send()
-
-    w_copy().wait_send()
-
-    @pl.loop(0, n_z)
-    def _(i):
-        sib_copy(i).wait_send()
-
-    @pl.loop(0, steps)
-    def _(t):
-        mate_copy(t).wait_send()
-
-        @pl.when(t < steps - 1)
-        def _():
-            rs_copy(t).wait_send()
 
 
 def body(n_alpha, n_z, coeffs, send_rows, a_source, a_sign, b_source, b_sign, integrals):
@@ -338,14 +405,16 @@
     V, DMA = pltpu.VMEM, pltpu.SemaphoreType.DMA
     blocks, half = 2 * n_z, n_z // 2
     scratch = [
-        V((slots, BLK), BF16), V((slots, BLK), BF16), V((blocks, BLK, slots), BF16),
+        V((slots, BLK), BF16), V((slots, BLK), BF16), V((slots, BLK), BF16),
+        V((5, BLK, BLK), BF16), V((5, slots, BLK), BF16), V((5, slots, BLK), BF16), V((blocks, BLK, slots), BF16),
         V((BLK, n_pairs), F32), V((BLK, n_pairs), F32), V((2 * NP, n_pairs), BF16),
         V((HALF, 2 * NP, slots), F32), V((NP, HALF, slots), BF16), V((NP, BLK, slots), BF16),
         V((slots, NP * BLK), BF16), V((NP * 2 * cols + 2 * LEAD, BLK), F32),
         V((cols // BLK, NP, BLK), I32), pltpu.SMEM((2, NP, BLK), I32),
         V((half, BLK, BLK), BF16), V((half, BLK, BLK), BF16), V((half, BLK, BLK), BF16), V((half, BLK, BLK), BF16),
         V((n_z, BLK, BLK), F32), V((n_z, BLK, BLK), F32), V((n_z, BLK, BLK), F32),
-        DMA((n_alpha,)), DMA((n_alpha,)), DMA((PARTS * n_z,)), DMA((PARTS * n_z,)),
+        DMA((n_alpha,)), DMA((n_alpha,)), DMA((5,)), DMA((5,)), DMA((2 * n_alpha,)), DMA((2 * n_alpha,)),
+        DMA((ROUND * HOPS,)), DMA((ROUND * HOPS,)),
         DMA((2 * n_z,)), DMA((2 * n_z,)),
         DMA, DMA, DMA((half,)), DMA((half,)), DMA((half,)), DMA((half,)), DMA((n_z,)), DMA((n_z,)), DMA((2,)),
     ]

time: 83.3 us -> 78.4 us (0.941)
  Pallas kernels: 81.7 us -> 76.8 us
    pallas_call x1, Pallas kernels: 81.7 us -> 76.8 us  [body(): pl.pallas_call(functools.partial(kernel, n_alpha, n_z), out_shape=jax.Sha...]
where the time goes in v3:
time: 78.4 us; the launch traced here: 78.2 us
  Pallas kernels  76.8 us (98%)
  local copies, waits for them, and re-layouts  1.38 us (2%)
    pallas_call x1, Pallas kernels, body(): pl.pallas_call(functools.partial(kernel, n_alpha, n_z), out_shape=jax.Sha...  76.8 us

profile of v3, /device:TPU:1, one launch (start us, length us, event | category | flops | bytes accessed | tf_op | source)
XLA Modules:
  0.0 78.2 jit_solution(18300853972401197420)
XLA Ops:
  0.0 76.8 %shard_map.73 = bf16[128,128]{1,0:T(8,128)(2,1)} custom-call(bf16[128,128]{1,0:T(8,128)(2,1)} %coeffs.1, s32[16,32]{1,0:T(8,128)} %send_rows.1, s32[256,128]{1,0:T(8,128)} %a_source.1, s32[256,128]{1,0:T(8,128)} %a_sign.1, s32[8,4096]{1,0:T(8,128)} %b_source.1, s32[8,4096]{1,0:T(8,128)} %b_sign.1, bf16[256,256]{1,0:T(8,128)(2,1)} %integrals.1), custom_call_target="tpu_custom_call" | custom-call | tf_op jit(solution)/shard_map/pallas_call | solution.py:421
  76.9 1.4 %copy.9 = bf16[128,128]{1,0:T(8,128)(2,1)} copy(bf16[128,128]{1,0:T(8,128)(2,1)} %shard_map.73) | data formatting | bytes 65536

commit v4 on v3

--- a/solution.py
+++ b/solution.py
@@ -25,12 +25,13 @@
 
 def kernel(
     n_alpha, n_z,
+    coeffs_hbm, send_rows_hbm, a_source_hbm, a_sign_hbm, b_source_hbm, b_sign_hbm, integrals_hbm,
+    out,
     coeffs, send_rows, a_source, a_sign, b_source, b_sign, integrals,
-    out,
     picked, received, hot, raw, far_picked, far_received, table, src_t, sgn_t, v16, w_raw, w_out, w_full, w_t, big, idx_v, idx_s,
     rs_in, rs_out, mate_in, mate_out, terms, sib_in, sib_out,
     pick_send, pick_recv, raw_send, raw_recv, far_send, far_recv, ring_send, ring_recv, half_send, half_recv, w_send, w_recv,
-    rs_send, rs_recv, mate_send, mate_recv, sib_send, sib_recv, idx_sem,
+    rs_send, rs_recv, mate_send, mate_recv, sib_send, sib_recv, idx_sem, load_sem,
 ):
     a = lax.axis_index("alpha")
     b = lax.axis_index("beta")
@@ -49,11 +50,22 @@
     other = z * 2 + 1 - core
 
     barrier = pltpu.get_barrier_semaphore()
+    for peer in (along(FAR), along(-FAR)):
+        pl.semaphore_signal(barrier, inc=1, device_id=(a, peer), device_id_type=MESH)
     for o in range(1, n_alpha):
         pl.semaphore_signal(barrier, inc=1, device_id=(lax.rem(a + o, n_alpha), b), device_id_type=MESH)
-    for peer in (along(FAR), along(-FAR), along(-2), up, down, other):
+    for peer in (along(-2), up, down, other):
         pl.semaphore_signal(barrier, inc=1, device_id=(a, peer), device_id_type=MESH)
 
+    given = (
+        (send_rows_hbm, send_rows), (coeffs_hbm, coeffs), (a_source_hbm, a_source), (a_sign_hbm, a_sign),
+        (integrals_hbm, integrals), (b_source_hbm, b_source), (b_sign_hbm, b_sign))
+    loads = [pltpu.make_async_copy(src, dst, load_sem.at[k]) for k, (src, dst) in enumerate(given)]
+    for load in loads:
+        load.start()
+
+    for load in loads[:2]:
+        load.wait()
     per = BLK // cap
     row_ids = lax.broadcasted_iota(I32, (BLK, BLK), 0)
     local = coeffs[...]
@@ -63,6 +75,8 @@
         hot[cut, :] = jnp.where(row_ids == line, 1.0, 0.0).T.astype(BF16)
         picked[cut, :] = jnp.dot(hot[cut, :], local, preferred_element_type=F32).astype(BF16)
 
+    for load in loads[2:]:
+        load.wait()
     src_t[...] = a_source[...].astype(F32).T
     sgn_t[...] = a_sign[...].astype(F32).T
     r16 = lax.broadcasted_iota(I32, (2 * NP, n_pairs), 0)
@@ -264,6 +278,15 @@
         def _():
             far_turn(1)
 
+        @pl.when(m == 4 * ROUND + 2)
+        def _():
+            far_wait(1)
+
+        for j in range(2, 5):
+            @pl.when(m == 4 * ROUND + 1 + j)
+            def _(j=j):
+                far_turn(j)
+
     side = jnp.where(z % 2 == 1, 1, -1)
     mate = lax.rem(z - side + n_z, n_z)
 
@@ -277,10 +300,6 @@
 
     for which in range(2):
         idx_copy(0, which).start()
-
-    far_wait(1)
-    for j in range(2, 5):
-        far_turn(j)
 
     @pl.loop(3 * HOPS - 4, n_z)
     def _(n):
@@ -405,6 +424,8 @@
     V, DMA = pltpu.VMEM, pltpu.SemaphoreType.DMA
     blocks, half = 2 * n_z, n_z // 2
     scratch = [
+        V((BLK, BLK), BF16), V(send_rows.shape, I32), V(a_source.shape, I32), V(a_sign.shape, I32),
+        V(b_source.shape, I32), V(b_sign.shape, I32), V(integrals.shape, BF16),
         V((slots, BLK), BF16), V((slots, BLK), BF16), V((slots, BLK), BF16),
         V((5, BLK, BLK), BF16), V((5, slots, BLK), BF16), V((5, slots, BLK), BF16), V((blocks, BLK, slots), BF16),
         V((BLK, n_pairs), F32), V((BLK, n_pairs), F32), V((2 * NP, n_pairs), BF16),
@@ -416,12 +437,12 @@
         DMA((n_alpha,)), DMA((n_alpha,)), DMA((5,)), DMA((5,)), DMA((2 * n_alpha,)), DMA((2 * n_alpha,)),
         DMA((ROUND * HOPS,)), DMA((ROUND * HOPS,)),
         DMA((2 * n_z,)), DMA((2 * n_z,)),
-        DMA, DMA, DMA((half,)), DMA((half,)), DMA((half,)), DMA((half,)), DMA((n_z,)), DMA((n_z,)), DMA((2,)),
+        DMA, DMA, DMA((half,)), DMA((half,)), DMA((half,)), DMA((half,)), DMA((n_z,)), DMA((n_z,)), DMA((2,)), DMA((7,)),
     ]
     return pl.pallas_call(
         functools.partial(kernel, n_alpha, n_z),
         out_shape=jax.ShapeDtypeStruct((BLK, BLK), BF16),
-        in_specs=[pl.BlockSpec(memory_space=V)] * 7,
+        in_specs=[pl.BlockSpec(memory_space=pl.ANY)] * 7,
         out_specs=pl.BlockSpec(memory_space=V),
         scratch_shapes=scratch,
         compiler_params=pltpu.CompilerParams(

time: 78.4 us -> 77.4 us (0.987)
  Pallas kernels: 76.8 us -> 75.8 us
    pallas_call x1, Pallas kernels: 76.8 us -> 75.8 us  [body(): pl.pallas_call(functools.partial(kernel, n_alpha, n_z), out_shape=jax.Sha...]
where the time goes in v4:
time: 77.4 us; the launch traced here: 77.2 us
  Pallas kernels  75.8 us (98%)
  local copies, waits for them, and re-layouts  1.38 us (2%)
    pallas_call x1, Pallas kernels, body(): pl.pallas_call(functools.partial(kernel, n_alpha, n_z), out_shape=jax.Sha...  75.8 us

profile of v4, /device:TPU:1, one launch (start us, length us, event | category | flops | bytes accessed | tf_op | source)
XLA Modules:
  0.0 77.2 jit_solution(14276906375954749775)
XLA Ops:
  0.0 75.8 %shard_map.73 = bf16[128,128]{1,0:T(8,128)(2,1)} custom-call(bf16[128,128]{1,0:T(8,128)(2,1)} %coeffs_hbm.1, s32[16,32]{1,0:T(8,128)} %send_rows_hbm.1, s32[256,128]{1,0:T(8,128)} %a_source_hbm.1, s32[256,128]{1,0:T(8,128)} %a_sign_hbm.1, s32[8,4096]{1,0:T(8,128)} %b_source_hbm.1, s32[8,4096]{1,0:T(8,128)} %b_sign_hbm.1, bf16[256,256]{1,0:T(8,128)(2,1)} %integrals_hbm.1), custom_call_target="tpu_custom_call" | custom-call | tf_op jit(solution)/shard_map/pallas_call | solution.py:442
  75.8 1.4 %copy.9 = bf16[128,128]{1,0:T(8,128)(2,1)} copy(bf16[128,128]{1,0:T(8,128)(2,1)} %shard_map.73) | data formatting | bytes 65536

commit v5 on v4

--- a/solution.py
+++ b/solution.py
@@ -1,4 +1,5 @@
 import functools
+import math
 
 import jax
 import jax.numpy as jnp
@@ -17,7 +18,6 @@
 ROUND = 2 * PARTS
 UNIT = 4
 LEAD = 8
-LAG = 5
 HOPS = 5
 FAR = 6
 GROUPS = ((0, 2), (2, 3))
@@ -52,8 +52,12 @@
     barrier = pltpu.get_barrier_semaphore()
     for peer in (along(FAR), along(-FAR)):
         pl.semaphore_signal(barrier, inc=1, device_id=(a, peer), device_id_type=MESH)
-    for o in range(1, n_alpha):
-        pl.semaphore_signal(barrier, inc=1, device_id=(lax.rem(a + o, n_alpha), b), device_id_type=MESH)
+    side_a = math.isqrt(n_alpha)
+    offsets = [(dy, dx) for dy in range(side_a) for dx in range(side_a) if dy or dx]
+    offsets.sort(key=lambda o: -sum(min(k, side_a - k) for k in o))
+    peers = [lax.rem(a // side_a + dy, side_a) * side_a + lax.rem(a % side_a + dx, side_a) for dy, dx in offsets]
+    for peer in peers:
+        pl.semaphore_signal(barrier, inc=1, device_id=(peer, b), device_id_type=MESH)
     for peer in (along(-2), up, down, other):
         pl.semaphore_signal(barrier, inc=1, device_id=(a, peer), device_id_type=MESH)
 
@@ -121,9 +125,8 @@
             send_sem=pick_send.at[to], recv_sem=pick_recv.at[frm],
             device_id=(to, b), device_id_type=MESH)
 
-    @pl.loop(1, n_alpha)
-    def _(o):
-        pick_copy(lax.rem(a + o, n_alpha), a).start()
+    for peer in peers:
+        pick_copy(peer, a).start()
 
     mine = pl.ds(pl.multiple_of(a * cap, cap), cap)
     received[mine, :] = picked[mine, :]
@@ -290,9 +293,17 @@
     side = jnp.where(z % 2 == 1, 1, -1)
     mate = lax.rem(z - side + n_z, n_z)
 
+    last = n_z - 1
+
+    def place(i):
+        own = jnp.logical_or(jnp.logical_and(i % 2 == 1, i >= 3), i == last - 1)
+        t_own = jnp.where(i >= last - 1, i - steps, (i - 3) // 2)
+        return own, jnp.where(own, t_own, jnp.where(i < 3, i, i // 2 + 1))
+
     def owner_of(i):
-        far = steps - 1 - i // 2
-        return lax.rem(jnp.where(i % 2 == 1, z + side * far, mate - side * far) + n_z, n_z)
+        own, t = place(i)
+        far = steps - 1 - t
+        return lax.rem(jnp.where(own, z + side * far, mate - side * far) + n_z, n_z)
 
     def idx_copy(i, which):
         chunk = owner_of(i) * 2 + jnp.where(which == 0, 1 - core, core)
@@ -331,21 +342,24 @@
     def rs_copy(t):
         return pltpu.make_async_remote_copy(
             src_ref=rs_out.at[t], dst_ref=rs_in.at[t], send_sem=rs_send.at[t], recv_sem=rs_recv.at[t],
-            device_id=(a, owner_of(2 * t + 1) * 2 + core), device_id_type=MESH)
-
-    def pass_on(t):
-        mate_copy(t).wait_recv()
-        rs_out[t] = (terms[2 * t + 1] + mate_in[t].astype(F32)).astype(BF16)
-        rs_copy(t).start()
+            device_id=(a, lax.rem(z + side * (steps - 1 - t) + n_z, n_z) * 2 + core), device_id_type=MESH)
 
     def chip_sum(i):
         sib_copy(i).wait_recv()
         terms[i] = terms[i] + sib_in[i]
 
-        @pl.when(i % 2 == 0)
-        def _():
-            mate_out[i // 2] = terms[i].astype(BF16)
-            mate_copy(i // 2).start()
+        own, t = place(i)
+
+        @pl.when(jnp.logical_not(own))
+        def _():
+            mate_out[t] = terms[i].astype(BF16)
+            mate_copy(t).start()
+
+        @pl.when(jnp.logical_and(own, i < last))
+        def _():
+            mate_copy(t).wait_recv()
+            rs_out[t] = (terms[i] + mate_in[t].astype(F32)).astype(BF16)
+            rs_copy(t).start()
 
     @pl.loop(0, n_z)
     def _(i):
@@ -361,10 +375,6 @@
         def _():
             chip_sum(i - 1)
 
-        @pl.when(jnp.logical_and(i % 2 == 1, i >= LAG))
-        def _():
-            pass_on((i - LAG) // 2)
-
         idx_copy(i, 1).wait()
         gather(1, terms.at[i])
 
@@ -372,9 +382,6 @@
         def _():
             idx_copy(i + 1, 1).start()
 
-    last = n_z - 1
-    for t in range((last - LAG) // 2 + 1, steps - 1):
-        pass_on(t)
     @pl.loop(1, n_alpha)
     def _(o):
         pick_copy(lax.rem(a + o, n_alpha), a).wait_send()

time: 77.4 us -> 76.3 us (0.986)
  Pallas kernels: 75.8 us -> 74.7 us
    pallas_call x1, Pallas kernels: 75.8 us -> 74.7 us  [body(): pl.pallas_call(functools.partial(kernel, n_alpha, n_z), out_shape=jax.Sha...]
where the time goes in v5:
time: 76.3 us; the launch traced here: 76.1 us
  Pallas kernels  74.7 us (98%)
  local copies, waits for them, and re-layouts  1.38 us (2%)
    pallas_call x1, Pallas kernels, body(): pl.pallas_call(functools.partial(kernel, n_alpha, n_z), out_shape=jax.Sha...  74.7 us

profile of v5, /device:TPU:1, one launch (start us, length us, event | category | flops | bytes accessed | tf_op | source)
XLA Modules:
  0.0 76.1 jit_solution(554897890265099579)
XLA Ops:
  0.0 74.7 %shard_map.73 = bf16[128,128]{1,0:T(8,128)(2,1)} custom-call(bf16[128,128]{1,0:T(8,128)(2,1)} %coeffs_hbm.1, s32[16,32]{1,0:T(8,128)} %send_rows_hbm.1, s32[256,128]{1,0:T(8,128)} %a_source_hbm.1, s32[256,128]{1,0:T(8,128)} %a_sign_hbm.1, s32[8,4096]{1,0:T(8,128)} %b_source_hbm.1, s32[8,4096]{1,0:T(8,128)} %b_sign_hbm.1, bf16[256,256]{1,0:T(8,128)(2,1)} %integrals_hbm.1), custom_call_target="tpu_custom_call" | custom-call | tf_op jit(solution)/shard_map/pallas_call | solution.py:449
  74.7 1.4 %copy.9 = bf16[128,128]{1,0:T(8,128)(2,1)} copy(bf16[128,128]{1,0:T(8,128)(2,1)} %shard_map.73) | data formatting | bytes 65536

commit v6 on v5

--- a/solution.py
+++ b/solution.py
@@ -224,7 +224,7 @@
 
     def mix(k):
         n = jnp.where(k == 7, 11, jnp.where(k == 10, 12, jnp.where(k < 7, k, jnp.where(k < 10, k - 1, k - 2))))
-        n = jnp.where(k > 12, k, n)
+        n = jnp.where(k > 10, jnp.where(k > 13, k - 5, k + 2), n)
         origin = origin_of(n)
         for h in range(2):
             half_copy(n, h, origin, 1 - core).wait_recv()

time: 76.3 us -> 75.7 us (level)
  no operation moved by 1% of the time
where the time goes in v6:
time: 75.7 us; the launch traced here: 75.5 us
  Pallas kernels  74.1 us (98%)
  local copies, waits for them, and re-layouts  1.38 us (2%)
    pallas_call x1, Pallas kernels, body(): pl.pallas_call(functools.partial(kernel, n_alpha, n_z), out_shape=jax.Sha...  74.1 us

profile of v6, /device:TPU:1, one launch (start us, length us, event | category | flops | bytes accessed | tf_op | source)
XLA Modules:
  0.0 75.5 jit_solution(8229412976372662382)
XLA Ops:
  0.0 74.1 %shard_map.73 = bf16[128,128]{1,0:T(8,128)(2,1)} custom-call(bf16[128,128]{1,0:T(8,128)(2,1)} %coeffs_hbm.1, s32[16,32]{1,0:T(8,128)} %send_rows_hbm.1, s32[256,128]{1,0:T(8,128)} %a_source_hbm.1, s32[256,128]{1,0:T(8,128)} %a_sign_hbm.1, s32[8,4096]{1,0:T(8,128)} %b_source_hbm.1, s32[8,4096]{1,0:T(8,128)} %b_sign_hbm.1, bf16[256,256]{1,0:T(8,128)(2,1)} %integrals_hbm.1), custom_call_target="tpu_custom_call" | custom-call | tf_op jit(solution)/shard_map/pallas_call | solution.py:449
  74.1 1.4 %copy.9 = bf16[128,128]{1,0:T(8,128)(2,1)} copy(bf16[128,128]{1,0:T(8,128)(2,1)} %shard_map.73) | data formatting | bytes 65536
